TPU v7x, 256 devices: a whole 4x4x8 slice. The times are simulated.
256 devices in a mesh: rep: 32 (over z, x_lo, core), shard: 8 (over x_hi, y).
Axes of the slice: x: 4 (x_hi: 2, x_lo: 2; x = x_hi * 2 + x_lo), y: 4, z: 8, core: 2. Of those that a mesh axis runs over, the one named last changes fastest.
Arguments:
- hidden_in: bfloat16 [49152, 8192], P(('rep', 'shard')), may hold values from -24 to 24
- queries: bfloat16 [49152, 4096], P(('rep', 'shard')), may hold values from -128 to 128
- keys: bfloat16 [49152, 512], P(('rep', 'shard')), may hold values from -5 to 5
- d_attn: bfloat16 [49152, 4096], P(('rep', 'shard')), may hold values from -6 to 6
- value_weight: bfloat16 [8192, 512], P('shard'), may hold values from -0.0625 to 0.0625
- pair_margin: float32 [256], P(('rep', 'shard')), may hold values from -30 to 30
- pair_chosen: int32 [256], P(('rep', 'shard')), may hold values from 0 to 1
Outputs:
- key_weight_grad: float32 [8192, 512], P('shard')
- value_weight_grad: float32 [8192, 512], P('shard')
All inputs are finite; a program needn't handle non-finite values.
Results may differ from a plain program's by a relative error of at most 0.015.
Values may be sent and summed in bfloat16 or wider, within the bound.
A program may use at most 128 MiB of HBM per device.

v0:
```python
import math

import jax
import jax.numpy as jnp
from jax import lax
from jax.sharding import PartitionSpec as P

HD = 128
LEN = 96


BETA_SPIN = 0.1
ROPE_BASE = 500000.0


def rotate_back(grad, positions):
    half = grad.shape[-1] // 2
    freqs = ROPE_BASE ** (-2.0 * jnp.arange(half, dtype=jnp.float32) / grad.shape[-1])
    angles = positions.astype(jnp.float32)[:, None] * freqs[None, :]
    cosine = jnp.cos(angles)[:, None, :]
    sine = jnp.sin(angles)[:, None, :]
    first = grad[..., :half]
    second = grad[..., half:]
    return jnp.concatenate(
        [first * cosine + second * sine, second * cosine - first * sine], axis=-1
    )


def token_weights(pair_margin, pair_chosen):
    strength = BETA_SPIN * jax.nn.sigmoid(-BETA_SPIN * pair_margin)
    first = strength * (2 * pair_chosen - 1).astype(jnp.float32)
    both = jnp.stack([first, -first], axis=1)
    return jnp.broadcast_to(both[:, :, None], (both.shape[0], 2, LEN)).reshape(-1)


def shards(hidden_in, queries, keys, d_attn, value_weight, pair_margin, pair_chosen):
    tok = hidden_in.shape[0]
    width = value_weight.shape[1]
    heads_kv = keys.shape[1] // HD
    group = queries.shape[1] // keys.shape[1]
    score_scale = 1.0 / math.sqrt(HD)
    position = jnp.arange(tok, dtype=jnp.int32)
    local_pos = position % LEN
    same = position[:, None] // LEN == position[None, :] // LEN
    allowed = same & (local_pos[None, :] <= local_pos[:, None])

    def reduce_grad(upstream):
        local = lax.psum_scatter(
            lax.dot_general(
                hidden_in, upstream, (((0,), (0,)), ((), ())), preferred_element_type=jnp.float32
            ).astype(jnp.bfloat16),
            "shard",
            scatter_dimension=0,
            tiled=True,
        ).astype(jnp.float32)
        return lax.psum(local, "rep")

    query_head_rows = queries.reshape(tok, heads_kv, group, HD)
    key_head_rows = keys.reshape(tok, heads_kv, HD)
    attention_scores = (
        jnp.einsum(
            "zvkj,ovj->vkzo", query_head_rows, key_head_rows, preferred_element_type=jnp.float32
        )
        * score_scale
    )
    attention_scores = jnp.where(allowed, attention_scores, -jnp.inf)
    top = jnp.max(attention_scores, axis=-1, keepdims=True)
    expo = jnp.exp(attention_scores - top)
    probs = expo / jnp.sum(expo, axis=-1, keepdims=True)
    probability_narrow = probs.astype(jnp.bfloat16)
    seq_weight = token_weights(pair_margin, pair_chosen)
    scaled = (d_attn.astype(jnp.float32) * seq_weight[:, None]).astype(jnp.bfloat16)
    scaled_query_heads = scaled.reshape(tok, heads_kv, group, HD)
    values_gradient = jnp.einsum(
        "fceq,efcb->qfb", probability_narrow, scaled_query_heads, preferred_element_type=jnp.float32
    )
    values_gradient = values_gradient.reshape(tok, width).astype(jnp.bfloat16)
    values = jnp.dot(
        hidden_in,
        lax.all_gather(value_weight, "shard", axis=0, tiled=True),
        preferred_element_type=jnp.float32,
    ).astype(jnp.bfloat16)
    value_head_rows = values.reshape(tok, heads_kv, HD)
    probability_gradient = jnp.einsum(
        "zvkj,ovj->vkzo", scaled_query_heads, value_head_rows, preferred_element_type=jnp.float32
    )
    inner = jnp.sum(probs * probability_gradient, axis=-1, keepdims=True)
    score_gradient = (probs * (probability_gradient - inner) * score_scale).astype(jnp.bfloat16)
    rotated_gradient = jnp.einsum(
        "fceq,efcb->qfb", score_gradient, query_head_rows, preferred_element_type=jnp.float32
    )
    d_keys = rotate_back(rotated_gradient, local_pos).reshape(tok, width).astype(jnp.bfloat16)
    key_grad = reduce_grad(d_keys)
    value_grad = reduce_grad(values_gradient)
    return (key_grad, value_grad)


def solution(mesh):
    placed = (
        P(("rep", "shard"), None),
        P(("rep", "shard"), None),
        P(("rep", "shard"), None),
        P(("rep", "shard"), None),
        P("shard", None),
        P(("rep", "shard")),
        P(("rep", "shard")),
    )
    return jax.shard_map(
        shards,
        mesh=mesh,
        in_specs=placed,
        out_specs=(P("shard", None), P("shard", None)),
        check_vma=False,
    )
```

profile of v0, /device:TPU:1, one launch (start us, length us, event | category | flops | bytes accessed | tf_op | source)
XLA Modules:
  0.0 512.9 jit_solution(13838150413472015553)
XLA Ops:
  7.2 0.0 copy-start
  7.2 0.0 all-gather.2.cloned.1.call-start
  7.2 0.7 all-gather.2.cloned.1.call-update
  7.9 0.0 reduce-scatter.5.cloned.1.call-start
  9.5 0.1 maximum_bitcast_fusion.1
  9.6 0.1 broadcast_in_dim.17
  9.6 0.1 broadcast_in_dim.18
  9.7 1.0 reshape.142
  10.7 0.0 copy-start.3
  10.7 2.0 fusion.15
  12.7 1.5 copy.39
  14.2 0.0 copy-done.3
  14.2 0.3 copy.38
  14.6 0.0 copy-start.2
  14.6 0.1 compare_and_fusion
  14.7 1.0 copy-done.2
  15.7 1.0 fusion.19
  16.8 1.9 fusion.42
  18.7 0.0 copy-start.1
  18.7 0.0 copy-start.4
  18.7 2.6 copy-done.1
  21.4 0.0 copy-done.4
  21.4 2.5 fusion.41
  23.9 5.7 %copy.31 = bf16[4,8,192,192]{3,1,0,2:T(8,128)(2,1)} copy(bf16[4,8,192,192]{2,3,1,0:T(8,128)(2,1)} %fusion.41) | data formatting | bytes 4718592 | tf_op jit(solution)/shard_map/convert_element_type | solution.py:70
  29.6 3.5 fusion.27
  33.0 0.0 copy-done
  33.0 5.6 %fusion.3 = bf16[8192,512]{0,1:T(8,128)(2,1)} fusion(bf16[192,8192]{1,0:T(8,128)(2,1)S(1)} %copy-done, bf16[4,24,8,128]{3,2,1,0:T(8,128)(2,1)S(1)} %fusion.27), kind=kOutput, calls=%fused_computation.5 | convolution fusion | flops 1614807040 | bytes 11730944 | tf_op jit(solution)/shard_map/dot_general | solution.py:49
  38.6 0.0 reduce-scatter.5.cloned.1.call-update
  38.7 0.2 reduce-scatter.3.cloned.1.call-start
  38.9 1.1 multiply_cosine_fusion
  40.0 86.2 %all-gather.2.cloned.1.call-done = bf16[8192,512]{1,0:T(8,128)(2,1)} async-done(((bf16[1024,512]{1,0:T(8,128)(2,1)}), bf16[8192,512]{1,0:T(8,128)(2,1)}) %all-gather.2.cloned.1.call-update) | async-done | bytes 8388624 | tf_op jit(solution)/shard_map/all_gather | solution.py:80
  126.2 5.2 %convolution_convert_fusion.2 = bf16[192,512]{1,0:T(8,128)(2,1)S(1)} fusion(bf16[192,8192]{1,0:T(8,128)(2,1)S(1)} %copy-done, bf16[8192,512]{1,0:T(8,128)(2,1)} %all-gather.2.cloned.1.call-done), kind=kOutput, calls=%fused_computation.31 | convolution fusion | flops 1610711040 | bytes 11730944 | tf_op jit(solution)/shard_map/dot_general | solution.py:78
  131.4 0.1 reshape.144
  131.4 5.1 %fusion.16 = f32[4,192,192,8]{2,1,3,0:T(8,128)} fusion(bf16[192,4,8,128]{3,2,1,0:T(8,128)(2,1)} %bitcast.77, bf16[192,4,128,1]{2,1,0,3:T(4,128)(2,1)S(1)} %bitcast.82), kind=kOutput, calls=%fused_computation.23 | convolution fusion | flops 301989888 | bytes 6488064 | tf_op jit(solution)/shard_map/zvkj,ovj->vkzo/dot_general | solution.py:84
  136.6 12.4 %fusion.21 = f32[192,4,128]{2,0,1:T(8,128)S(1)} fusion(bf16[192,4,8,128]{3,2,1,0:T(8,128)(2,1)} %bitcast.79, f32[4,192,192,8]{2,1,3,0:T(8,128)} %fusion.16, f32[4,8,192,192]{2,3,1,0:T(8,128)} %copy-done.1, f32[4,8,192]{2,1,0:T(8,128)} %copy-done.4), kind=kOutput, calls=%fused_computation.28 | convolution fusion | flops 310253760 | bytes 11427840 | tf_op jit(solution)/shard_map/fceq,efcb->qfb/dot_general | solution.py:89
  148.9 1.1 add_convert_fusion
  150.1 5.7 %fusion.2 = bf16[8192,512]{0,1:T(8,128)(2,1)} fusion(bf16[192,8192]{1,0:T(8,128)(2,1)S(1)} %copy-done, bf16[192,4,64]{2,0,1:T(8,128)(2,1)S(1)} %get-tuple-element.9, bf16[192,4,64]{2,0,1:T(8,128)(2,1)S(1)} %get-tuple-element.8), kind=kOutput, calls=%fused_computation.4 | convolution fusion | flops 1615200256 | bytes 11730944 | tf_op jit(solution)/shard_map/dot_general | solution.py:49
  155.8 0.0 reduce-scatter.3.cloned.1.call-update
  155.8 91.9 %reduce-scatter.5.cloned.1.call-done = bf16[1024,512]{0,1:T(8,128)(2,1)} async-done(((bf16[8192,512]{0,1:T(8,128)(2,1)}), bf16[1024,512]{0,1:T(8,128)(2,1)}) %reduce-scatter.5.cloned.1.call-update) | async-done | bytes 1048592 | tf_op jit(solution)/shard_map/reduce_scatter | solution.py:48
  247.8 122.3 %reduce-scatter.3.cloned.1.call-done = bf16[1024,512]{0,1:T(8,128)(2,1)} async-done(((bf16[8192,512]{0,1:T(8,128)(2,1)}), bf16[1024,512]{0,1:T(8,128)(2,1)}) %reduce-scatter.3.cloned.1.call-update) | async-done | bytes 1048592 | tf_op jit(solution)/shard_map/reduce_scatter | solution.py:48
  370.1 130.6 %all-reduce.2 = (f32[1024,512]{0,1:T(8,128)}, f32[1024,512]{0,1:T(8,128)}) all-reduce(bf16[1024,512]{0,1:T(8,128)(2,1)} %reduce-scatter.3.cloned.1.call-done, bf16[1024,512]{0,1:T(8,128)(2,1)} %reduce-scatter.5.cloned.1.call-done), channel_id=1, replica_groups=mesh['rep'=32,'shard'=8] {'rep'}, use_global_device_ids=true, to_apply=%region_4.5 | all-reduce | flops 1048576 | bytes 6291456 | tf_op jit(solution)/shard_map/psum | solution.py:56
  500.7 2.9 copy.25
  503.5 2.9 copy.26
  (3 shorter events, 0.0 us)
Async XLA Ops:
  7.2 25.9 %copy-start = (bf16[192,8192]{1,0:T(8,128)(2,1)S(1)}, bf16[192,8192]{1,0:T(8,128)(2,1)}, u32[]{:S(2)}) copy-start(bf16[192,8192]{1,0:T(8,128)(2,1)} %param.7) | copy-start | bytes 9437188
  7.2 119.0 %all-gather.2.cloned.1.call-start = ((), (), s32[]{:S(2)}) async-start(), calls=%async_computation.2 | async-start | bytes 9437184 | tf_op jit(solution)/shard_map/all_gather | solution.py:80
  7.9 239.8 %reduce-scatter.5.cloned.1.call-start = ((), (), s32[]{:S(2)}) async-start(), calls=%async_computation.4 | async-start | bytes 9437184 | tf_op jit(solution)/shard_map/reduce_scatter | solution.py:48
  10.7 3.5 copy-start.3
  14.6 1.1 copy-start.2
  18.7 2.6 copy-start.1
  18.7 2.6 copy-start.4
  38.7 331.4 %reduce-scatter.3.cloned.1.call-start = ((), (), s32[]{:S(2)}) async-start(), calls=%async_computation.3 | async-start | bytes 9437184 | tf_op jit(solution)/shard_map/reduce_scatter | solution.py:48
Sparse Core Ops, SparseCore 0:
  10.7 115.5 all-gather.1
  130.3 117.3 reduce-scatter.4
  252.4 117.5 reduce-scatter.2
where the time goes:
time: 515 us; the launch traced here: 513 us
  waiting for transfers between devices  301 us (58%)
  blocking collectives  131 us (25%)
  matrix products  38.5 us (7%)
  local copies, waits for them, and re-layouts  18.1 us (4%)
  between operations  15.4 us (3%)
  other arithmetic  8.88 us (2%)
    reduce_scatter x2, waiting for transfers between devices, reduce_grad(): lax.psum_scatter(lax.dot_general(hidden_in, upstream, (((0,), (0,)), ((),...  214 us
    psum x1, blocking collectives, reduce_grad(): return lax.psum(local, 'rep')  131 us
    all_gather x1, waiting for transfers between devices, shards(): lax.all_gather(value_weight, 'shard', axis=0, tiled=True)  86.2 us
    dot_general x1, matrix products, shards(): jnp.einsum('fceq,efcb->qfb', score_gradient, query_head_rows, preferred_e...  12.4 us
    dot_general x2, matrix products, reduce_grad(): lax.dot_general(hidden_in, upstream, (((0,), (0,)), ((), ())), preferred_...  11.3 us
    unnamed x14, local copies, waits for them, and re-layouts  11.2 us
  transfers between devices with their start and end apart: 3, of which 3 were waited for; matrix products, arithmetic and copies ran while one was open for 11% of the time, Pallas kernels for 0%

commit v1 on v0

v1 whole, which is shorter than its diff:
```python
import functools
import math

import jax
import jax.numpy as jnp
import numpy as np
from jax import lax
from jax.experimental import pallas as pl
from jax.experimental.pallas import tpu as pltpu
from jax.sharding import PartitionSpec as P

HD = 128
LEN = 96
TOK = 192
HEADS = 4
GROUP = 8
COLS = GROUP * LEN
BETA_SPIN = 0.1
ROPE_BASE = 500000.0
SCALE = 1.0 / math.sqrt(HD)
MESH = pl.DeviceIdType.MESH
BF = jnp.bfloat16
F32 = jnp.float32


class Links:
    def __init__(self, send, recv):
        self.send, self.recv, self.count, self.all = send, recv, 0, []

    def start(self, src, dst, device):
        copy = pltpu.make_async_remote_copy(
            src_ref=src,
            dst_ref=dst,
            send_sem=self.send.at[self.count],
            recv_sem=self.recv.at[self.count],
            device_id=device,
            device_id_type=MESH,
        )
        copy.start()
        self.count += 1
        self.all.append(copy)
        return copy


def kernel(
    margin, chosen, cosine, sine, q, k, da, x_hbm, wv_hbm,
    out_k, out_v,
    xc, wc, probs, sc, qc, acc, vr, vals, dvb, dkb,
    pv, rz0, rz, rvx, vx, rvy,
    pa, ra1, ra2, qa, ra3, ra4,
    pb, rb1, rb2, qb, rb3, rb4,
    kz, rkz, send, recv, local,
):
    rep, shard = lax.axis_index("rep"), lax.axis_index("shard")
    z, l, c = rep // 4, (rep // 2) % 2, rep % 2
    h, y = shard // 4, shard % 4
    x = 2 * h + l

    def dev(xx, yy, zz, cc):
        return (zz * 4 + (xx % 2) * 2 + cc, (xx // 2) * 4 + yy)

    def at_x(d):
        return dev((x + d) % 4, y, z, c)

    def at_y(d):
        return dev(x, (y + d) % 4, z, c)

    def at_z(d):
        return dev(x, y, (z + d) % 8, c)

    sib = dev(x, y, z, 1 - c)
    outer = dev(3 - x, y, z, c)
    inner = dev(2 * h + 1 - l, y, z, c)

    peers = [sib] + [at_x(d) for d in (1, 2, 3)] + [at_y(d) for d in (1, 2, 3)] + [at_z(d) for d in range(1, 8)]
    barrier = pltpu.get_barrier_semaphore()
    for peer in peers:
        pl.semaphore_signal(barrier, inc=1, device_id=peer, device_id_type=MESH)
    pl.semaphore_wait(barrier, len(peers))

    links = Links(send, recv)

    def rows_of(quarter):
        return pl.ds(pl.multiple_of(quarter * 512 + c * 256, 256), 256)

    own_copies = []

    def keep(src, dst):
        copy = pltpu.make_async_copy(src, dst, local.at[len(own_copies)])
        copy.start()
        own_copies.append(copy)

    first = 1 - l
    w_outer = {0: links.start(wv_hbm.at[rows_of(first)], wc.at[(2 * h + first) * 4 + y], outer)}
    w_y = {}
    for quarter in (first, l):
        for d in (1, 3, 2):
            w_y[d, quarter is first] = links.start(
                wv_hbm.at[rows_of(quarter)], wc.at[(2 * h + quarter) * 4 + y], at_y(d)
            )
    xs = []
    for xx in range(4):
        for yy in range(4):
            base = (xx // 2) * 4096 + yy * 1024 + (xx % 2) * 512
            theirs = pl.ds(pl.multiple_of(base + (1 - c) * 256, 256), 256)
            mine = pl.ds(pl.multiple_of(base + c * 256, 256), 256)
            xs.append(links.start(x_hbm.at[:, theirs], xc.at[xx * 4 + yy, c], sib))
            keep(x_hbm.at[:, mine], xc.at[xx * 4 + yy, c])
    for quarter in range(2):
        keep(wv_hbm.at[rows_of(quarter)], wc.at[(2 * h + quarter) * 4 + y])

    strength = BETA_SPIN / (1.0 + jnp.exp(BETA_SPIN * margin[...]))
    weight = strength * (2 * chosen[...] - 1).astype(F32)
    s_pos = lax.broadcasted_iota(jnp.int32, (LEN, COLS), 0)
    t_pos = lax.broadcasted_iota(jnp.int32, (LEN, COLS), 1) % LEN
    allowed = s_pos <= t_pos

    def forward(g, carry):
        for seq in range(2):
            unit = 2 * g + seq
            rows = pl.ds(seq * LEN, LEN)
            w = weight if seq == 0 else -weight
            for head in range(GROUP):
                cols = pl.ds(pl.multiple_of(g * GROUP * HD + head * HD, HD), HD)
                span = pl.ds(head * LEN, LEN)
                qc[unit, span, :] = q[rows, cols]
                sc[unit, span, :] = (da[rows, cols].astype(F32) * w).astype(BF)
            kcols = pl.ds(pl.multiple_of(g * HD, HD), HD)
            scores = lax.dot_general(
                k[rows, kcols], qc[unit], (((1,), (1,)), ((), ())), preferred_element_type=F32
            ) * SCALE
            scores = jnp.where(allowed, scores, -jnp.inf)
            top = jnp.max(scores, axis=0, keepdims=True)
            expo = jnp.exp(scores - top)
            p = expo / jnp.sum(expo, axis=0, keepdims=True)
            probs[unit] = p
            dv = jnp.dot(p.astype(BF), sc[unit], preferred_element_type=F32)
            dvb[c, rows, kcols] = dv.astype(BF)
        return carry

    lax.fori_loop(0, HEADS, forward, 0)
    dv_copy = links.start(dvb.at[c], dvb.at[c], sib)
    for copy in own_copies:
        copy.wait()
    for copy in xs:
        copy.wait_recv()
    dv_copy.wait_recv()

    def partial_grad(d, store):
        dt = jnp.transpose(d[...].reshape(2 * TOK, 512).astype(F32)).astype(BF)

        def body(i, carry):
            out = jnp.dot(dt, xc[i].reshape(2 * TOK, 256), preferred_element_type=F32).astype(BF)
            for zz in range(8):
                cb, rh = zz // 2, zz % 2
                store(i, zz, out[cb * 128 : (cb + 1) * 128, rh * 128 : (rh + 1) * 128])
            return carry

        lax.fori_loop(0, 16, body, 0)

    def store_v(i, zz, block):
        pv[zz, i] = block

    partial_grad(dvb, store_v)

    half_a, half_b = pl.ds(0, 8), pl.ds(8, 8)

    def add(dst, src, start, count):
        def body(i, carry):
            dst[start + i] = (dst[start + i].astype(F32) + src[i].astype(F32)).astype(BF)
            return carry

        lax.fori_loop(0, count, body, 0)

    def z_at(d):
        return pv.at[(z + d) % 8]

    z_copies = {}

    def z_step(step):
        for di, sign in ((0, 1), (1, -1)):
            lead, other = (half_a, half_b) if sign == 1 else (half_b, half_a)
            lead0, other0 = (0, 8) if sign == 1 else (8, 0)
            far = z_at(sign * (4 - step) + 8)
            near = z_at(sign * (3 - step) + 8)
            if step > 0:
                z_copies[di, step - 1, 0].wait_recv()
                add(far, rz.at[di, step - 1, half_a], lead0, 8)
            z_copies[di, step, 0] = links.start(far.at[lead], rz.at[di, step, half_a], at_z(sign + 8))
            if step < 3:
                if step > 0:
                    z_copies[di, step - 1, 1].wait_recv()
                    add(near, rz.at[di, step - 1, half_b], other0, 8)
                z_copies[di, step, 1] = links.start(near.at[other], rz.at[di, step, half_b], at_z(sign + 8))

    z_step(0)

    def values_add(count, place, init=False):
        def body(i, carry):
            j = place(i)
            part = jnp.dot(
                xc[j].reshape(2 * TOK, 256), wc[j], preferred_element_type=F32
            ).reshape(2, TOK, 512)
            acc[...] += part
            return carry

        lax.fori_loop(0, count, body, 0)

    def pass_outer(d):
        w_y[d, True].wait_recv()
        block = wc.at[(2 * h + first) * 4 + (y + 4 - d) % 4]
        w_outer[d] = links.start(block, block, outer)

    w_inner = {}

    def pass_inner(d):
        w_outer[d].wait_recv()
        block = wc.at[(2 * (1 - h) + l) * 4 + (y + 4 - d) % 4]
        w_inner[d] = links.start(block, block, inner)

    acc[...] = jnp.zeros_like(acc)
    pass_inner(0)
    pass_outer(1)
    pass_outer(3)
    pass_outer(2)
    values_add(2, lambda i: (2 * h + i) * 4 + y)
    pass_inner(1)
    z_step(1)
    pass_inner(3)
    for d in (1, 3, 2):
        w_y[d, False].wait_recv()
    values_add(6, lambda i: (2 * h + i % 2) * 4 + (y + 1 + i // 2) % 4)
    pass_inner(2)
    values_add(4, lambda i: (2 * (1 - h) + l) * 4 + i)
    for d in (0, 1, 3, 2):
        w_inner[d].wait_recv()
    values_add(4, lambda i: (2 * (1 - h) + 1 - l) * 4 + i)
    value_copy = links.start(acc.at[1 - c], vr, sib)
    z_step(2)
    value_copy.wait_recv()
    vals[...] = (acc[c] + vr[...]).astype(BF)

    def backward(g, carry):
        for seq in range(2):
            unit = 2 * g + seq
            rows = pl.ds(seq * LEN, LEN)
            kcols = pl.ds(pl.multiple_of(g * HD, HD), HD)
            dp = lax.dot_general(
                vals[rows, kcols], sc[unit], (((1,), (1,)), ((), ())), preferred_element_type=F32
            )
            p = probs[unit]
            mean = jnp.sum(p * dp, axis=0, keepdims=True)
            ds = (p * (dp - mean) * SCALE).astype(BF)
            rot = jnp.dot(ds, qc[unit], preferred_element_type=F32)
            swapped = jnp.concatenate([rot[:, HD // 2 :], rot[:, : HD // 2]], axis=1)
            dkb[c, rows, kcols] = (rot * cosine[...] + swapped * sine[...]).astype(BF)
        return carry

    lax.fori_loop(0, HEADS, backward, 0)
    dk_copy = links.start(dkb.at[c], dkb.at[c], sib)
    dk_copy.wait_recv()

    def store_k(i, zz, block):
        pa[i // 4, i % 4, zz] = block[:64]
        pb[i % 4, i // 4, zz] = block[64:]

    partial_grad(dkb, store_k)

    def ring_start(at, me, p, r1, r2, n):
        lo, hi = pl.ds(0, n // 2), pl.ds(n // 2, n // 2)
        far, up, down = p.at[(me + 2) % 4], p.at[(me + 1) % 4], p.at[(me + 3) % 4]
        return {
            "up1": links.start(far.at[lo], r1.at[0], at(1)),
            "down1": links.start(far.at[hi], r1.at[1], at(3)),
            "up2": links.start(up.at[hi], r2.at[0, hi], at(1)),
            "down2": links.start(down.at[lo], r2.at[1, lo], at(3)),
        }

    def add2(dst, src, start, count):
        def body(i, carry):
            dst[start + i] = (dst[start + i].astype(F32) + src[i].astype(F32)).astype(BF)
            return carry

        lax.fori_loop(0, count, body, 0)

    def ring_pass(copies, at, me, p, r1, r2, n):
        lo, hi = pl.ds(0, n // 2), pl.ds(n // 2, n // 2)
        up, down = p.at[(me + 1) % 4], p.at[(me + 3) % 4]
        copies["up1"].wait_recv()
        add2(up, r1.at[0], 0, n // 2)
        copies["up3"] = links.start(up.at[lo], r2.at[0, lo], at(1))
        copies["down1"].wait_recv()
        add2(down, r1.at[1], n // 2, n // 2)
        copies["down3"] = links.start(down.at[hi], r2.at[1, hi], at(3))

    def ring_end(copies, me, p, r2, n, store):
        for name in ("up2", "down2", "up3", "down3"):
            copies[name].wait_recv()

        def body(i, carry):
            store(i, p[me, i].astype(F32) + r2[0, i].astype(F32) + r2[1, i].astype(F32))
            return carry

        lax.fori_loop(0, n, body, 0)

    a1 = ring_start(at_x, x, pa, ra1, ra2, 4)
    b1 = ring_start(at_y, y, pb, rb1, rb2, 4)
    z_step(3)
    ring_pass(a1, at_x, x, pa, ra1, ra2, 4)
    ring_pass(b1, at_y, y, pb, rb1, rb2, 4)

    z_copies[0, 2, 1].wait_recv()
    z_copies[1, 2, 1].wait_recv()
    z_copies[0, 3, 0].wait_recv()
    z_copies[1, 3, 0].wait_recv()
    mine = z_at(0)

    def v_sum(i, carry):
        lead_up, other_up = rz[0, 3, i % 8], rz[0, 2, 8 + i % 8]
        lead_down, other_down = rz[1, 3, i % 8], rz[1, 2, 8 + i % 8]
        in_a = i < 8
        up = jnp.where(in_a, lead_up.astype(F32), other_up.astype(F32))
        down = jnp.where(in_a, other_down.astype(F32), lead_down.astype(F32))
        mine[i] = (mine[i].astype(F32) + up + down).astype(BF)
        return carry

    lax.fori_loop(0, 16, v_sum, 0)
    vx_copies = [
        links.start(mine.at[pl.ds(((x + d) % 4) * 4, 4)], rvx.at[d - 1], at_x(d)) for d in (1, 2, 3)
    ]

    def store_qa(i, total):
        qa[i] = total.astype(BF)

    def store_qb(i, total):
        qb[i] = total.astype(BF)

    ring_end(a1, x, pa, ra2, 4, store_qa)
    a2 = ring_start(at_y, y, qa, ra3, ra4, 8)
    ring_end(b1, y, pb, rb2, 4, store_qb)
    b2 = ring_start(at_x, x, qb, rb3, rb4, 8)

    for copy in vx_copies:
        copy.wait_recv()

    def vx_sum(i, carry):
        total = mine[x * 4 + i].astype(F32)
        for d in range(3):
            total += rvx[d, i].astype(F32)
        vx[i] = total.astype(BF)
        return carry

    lax.fori_loop(0, 4, vx_sum, 0)
    vy_copies = [links.start(vx.at[(y + d) % 4], rvy.at[d - 1], at_y(d)) for d in (1, 2, 3)]

    ring_pass(a2, at_y, y, qa, ra3, ra4, 8)
    ring_pass(b2, at_x, x, qb, rb3, rb4, 8)

    def spot(ref, zz, ll, cc):
        row = ll * 512 + cc * 256 + (zz % 2) * 128
        return ref.at[
            pl.ds(pl.multiple_of(row, 128), 128), pl.ds(pl.multiple_of((zz // 2) * 128, 128), 128)
        ]

    def gather_start(ref, total):
        place = spot(ref, z, l, c)
        place[...] = jnp.transpose(total).astype(BF)
        state = {"z": {}, "in": {}, "sib": {}}
        for d in (4, 3, 5, 2, 6, 1, 7):
            state["z"][d] = links.start(place, place, at_z(d))
        state["in"][0] = links.start(place, place, inner)
        state["sib"][0, 0] = links.start(place, place, sib)
        return state

    def gather_mid(ref, state):
        for d in (1, 7, 2, 6, 3, 5, 4):
            state["z"][d].wait_recv()
            place = spot(ref, (z + 8 - d) % 8, l, c)
            state["in"][d] = links.start(place, place, inner)
            state["sib"][d, 0] = links.start(place, place, sib)

    def gather_end(ref, state):
        for d in (0, 1, 7, 2, 6, 3, 5, 4):
            state["in"][d].wait_recv()
            place = spot(ref, (z + 8 - d) % 8, 1 - l, c)
            state["sib"][d, 1] = links.start(place, place, sib)

    for copy in vy_copies:
        copy.wait_recv()
    total_v = vx[y].astype(F32)
    for d in range(3):
        total_v += rvy[d].astype(F32)
    gv = gather_start(out_v, total_v)

    def store_za(i, total):
        kz[i, pl.ds(0, 64), :] = total.astype(BF)

    def store_zb(i, total):
        kz[i, pl.ds(64, 64), :] = total.astype(BF)

    ring_end(a2, y, qa, ra4, 8, store_za)
    ring_end(b2, x, qb, rb4, 8, store_zb)
    kz_copies = [links.start(kz.at[(z + d) % 8], rkz.at[d - 1], at_z(d)) for d in range(1, 8)]
    gather_mid(out_v, gv)
    total_k = kz[z].astype(F32)
    for d in range(7):
        kz_copies[d].wait_recv()
        total_k += rkz[d].astype(F32)
    gk = gather_start(out_k, total_k)
    gather_end(out_v, gv)
    gather_mid(out_k, gk)
    gather_end(out_k, gk)
    for state in (gv, gk):
        for copy in state["sib"].values():
            copy.wait_recv()
    for copy in links.all:
        copy.wait_send()


def rotary_tables():
    half = HD // 2
    freqs = np.float32(ROPE_BASE) ** (-2.0 * np.arange(half, dtype=np.float32) / HD)
    angles = np.arange(LEN, dtype=np.float32)[:, None] * freqs.astype(np.float32)[None, :]
    cosine, sine = np.cos(angles), np.sin(angles)
    return (
        np.concatenate([cosine, cosine], axis=1).astype(np.float32),
        np.concatenate([sine, -sine], axis=1).astype(np.float32),
    )


def shards(hidden_in, queries, keys, d_attn, value_weight, pair_margin, pair_chosen):
    cosine, sine = rotary_tables()
    vmem = pl.BlockSpec(memory_space=pltpu.VMEM)
    anywhere = pl.BlockSpec(memory_space=pl.ANY)
    block = (128, 128)
    key_grad, value_grad = pl.pallas_call(
        kernel,
        name="projection_grads",
        out_shape=[jax.ShapeDtypeStruct((1024, 512), BF)] * 2,
        in_specs=[vmem] * 7 + [anywhere] * 2,
        out_specs=[vmem] * 2,
        scratch_shapes=[
            pltpu.VMEM((16, 2, TOK, 256), BF),
            pltpu.VMEM((16, 256, 512), BF),
            pltpu.VMEM((8, LEN, COLS), F32),
            pltpu.VMEM((8, COLS, HD), BF),
            pltpu.VMEM((8, COLS, HD), BF),
            pltpu.VMEM((2, TOK, 512), F32),
            pltpu.VMEM((TOK, 512), F32),
            pltpu.VMEM((TOK, 512), BF),
            pltpu.VMEM((2, TOK, 512), BF),
            pltpu.VMEM((2, TOK, 512), BF),
            pltpu.VMEM((8, 16) + block, BF),
            pltpu.VMEM((1, 128), BF),
            pltpu.VMEM((2, 4, 16) + block, BF),
            pltpu.VMEM((3, 4) + block, BF),
            pltpu.VMEM((4,) + block, BF),
            pltpu.VMEM((3,) + block, BF),
        ]
        + [
            pltpu.VMEM((4, 4, 8, 64, 128), BF),
            pltpu.VMEM((2, 2, 8, 64, 128), BF),
            pltpu.VMEM((2, 4, 8, 64, 128), BF),
            pltpu.VMEM((4, 8, 64, 128), BF),
            pltpu.VMEM((2, 4, 64, 128), BF),
            pltpu.VMEM((2, 8, 64, 128), BF),
        ]
        * 2
        + [
            pltpu.VMEM((8,) + block, BF),
            pltpu.VMEM((7,) + block, BF),
            pltpu.SemaphoreType.DMA((160,)),
            pltpu.SemaphoreType.DMA((160,)),
            pltpu.SemaphoreType.DMA((18,)),
        ],
        compiler_params=pltpu.CompilerParams(
            collective_id=0, has_side_effects=True, vmem_limit_bytes=58 * 2**20
        ),
    )(
        pair_margin.reshape(1, 1),
        pair_chosen.reshape(1, 1),
        jnp.asarray(cosine),
        jnp.asarray(sine),
        queries,
        keys,
        d_attn,
        hidden_in,
        value_weight,
    )
    return key_grad.astype(F32), value_grad.astype(F32)


def solution(mesh):
    placed = (
        P(("rep", "shard"), None),
        P(("rep", "shard"), None),
        P(("rep", "shard"), None),
        P(("rep", "shard"), None),
        P("shard", None),
        P(("rep", "shard")),
        P(("rep", "shard")),
    )
    return jax.shard_map(
        shards,
        mesh=mesh,
        in_specs=placed,
        out_specs=(P("shard", None), P("shard", None)),
        check_vma=False,
    )
```

time: 515 us -> 126 us (0.24)
  waiting for transfers between devices: 301 us -> 0 us
  blocking collectives: 131 us -> 0 us
  Pallas kernels: 0 us -> 120 us
  matrix products: 38.5 us -> 0 us
  local copies, waits for them, and re-layouts: 18.1 us -> 0.01 us
  between operations: 15.4 us -> 1.94 us
    reduce_scatter x2 -> x0, waiting for transfers between devices: 214 us -> none  [reduce_grad(): lax.psum_scatter(lax.dot_general(hidden_in, upstream, (((0,), (0,)), ((),...]
    psum x1 -> x0, blocking collectives: 131 us -> none  [reduce_grad(): return lax.psum(local, 'rep')]
    pallas_call x0 -> x1, Pallas kernels: none -> 120 us  [shards(): pl.pallas_call(kernel, name='projection_grads', out_shape=[jax.ShapeDtype...]
    all_gather x1 -> x0, waiting for transfers between devices: 86.2 us -> none  [shards(): lax.all_gather(value_weight, 'shard', axis=0, tiled=True)]
    dot_general x7 -> x0, matrix products: 38.5 us -> none  [the longest x1 12.4 us: shards(): jnp.einsum('fceq,efcb->qfb', score_gradient, query_head_rows, preferred_e...]
    unnamed x14 -> x2, local copies, waits for them, and re-layouts: 11.2 us -> 0.01 us
    convert_element_type x1 -> x0, local copies, waits for them, and re-layouts: 5.71 us -> none  [shards(): probability_narrow = probs.astype(jnp.bfloat16)]
  transfers between devices with their start and end apart: 3 -> 0, of which waited for: 3 -> 0; matrix products, arithmetic and copies ran while one was open for 11% -> 0% of each run, Pallas kernels for 0% -> 0%
where the time goes in v1:
time: 126 us
  Pallas kernels  120 us (95%)
  other arithmetic  4.54 us (4%)
  between operations  1.94 us (2%)
    pallas_call x1, Pallas kernels, shards(): pl.pallas_call(kernel, name='projection_grads', out_shape=[jax.ShapeDtype...  120 us
    convert_element_type x2, other arithmetic, shards(): return (key_grad.astype(F32), value_grad.astype(F32))  4.54 us

profile of v1, /device:TPU:1, one launch (start us, length us, event | category | flops | bytes accessed | tf_op | source)
XLA Modules:
  0.0 126.1 jit_solution(3784496096813589660)
XLA Ops:
  1.9 119.6 %projection_grads.1 = (bf16[1024,512]{1,0:T(8,128)(2,1)}, bf16[1024,512]{1,0:T(8,128)(2,1)}) custom-call(f32[1,1]{1,0:T(1,128)} %bitcast.2.margin, s32[1,1]{1,0:T(1,128)} %bitcast.3.chosen, f32[96,128]{1,0:T(8,128)} %constant.4.clone.cosine, f32[96,128]{1,0:T(8,128)} %constant.5.clone.sine, bf16[192,4096]{1,0:T(8,128)(2,1)} %q.1, bf16[192,512]{1,0:T(8,128)(2,1)} %k.1, ...), custom_call_target="tpu_custom_call" | custom-call | tf_op jit(solution)/shard_map/projection_grads/pallas_call | solution.py:436
  121.6 0.0 copy-start
  121.6 2.9 %convert_element_type.6 = f32[1024,512]{1,0:T(8,128)} convert(bf16[1024,512]{1,0:T(8,128)(2,1)} %get-tuple-element.4) | non-fusion elementwise | flops 524288 | bytes 3145728 | tf_op jit(solution)/shard_map/convert_element_type | solution.py:490
  124.5 0.0 copy-done
  124.5 1.6 %convert_element_type.7 = f32[1024,512]{1,0:T(8,128)} convert(bf16[1024,512]{1,0:T(8,128)(2,1)S(1)} %copy-done) | non-fusion elementwise | flops 524288 | bytes 3145728 | tf_op jit(solution)/shard_map/convert_element_type | solution.py:490
Async XLA Ops:
  121.6 2.9 %copy-start = (bf16[1024,512]{1,0:T(8,128)(2,1)S(1)}, bf16[1024,512]{1,0:T(8,128)(2,1)}, u32[]{:S(2)}) copy-start(bf16[1024,512]{1,0:T(8,128)(2,1)} %get-tuple-element.5) | copy-start | bytes 3145732

commit v2 on v1

v2 whole, which is shorter than its diff:
```python
import functools
import math

import jax
import jax.numpy as jnp
import numpy as np
from jax import lax
from jax.experimental import pallas as pl
from jax.experimental.pallas import tpu as pltpu
from jax.sharding import PartitionSpec as P

HD = 128
LEN = 96
TOK = 192
HEADS = 4
GROUP = 8
COLS = GROUP * LEN
BETA_SPIN = 0.1
ROPE_BASE = 500000.0
SCALE = 1.0 / math.sqrt(HD)
MESH = pl.DeviceIdType.MESH
BF = jnp.bfloat16
F32 = jnp.float32


class Links:
    def __init__(self, send, recv):
        self.send, self.recv, self.count, self.all = send, recv, 0, []

    def start(self, src, dst, device):
        copy = pltpu.make_async_remote_copy(
            src_ref=src,
            dst_ref=dst,
            send_sem=self.send.at[self.count],
            recv_sem=self.recv.at[self.count],
            device_id=device,
            device_id_type=MESH,
        )
        copy.start()
        self.count += 1
        self.all.append(copy)
        return copy


def add_blocks(dst, src, count):
    for i in range(count):
        dst[i] = (dst[i].astype(F32) + src[i].astype(F32)).astype(BF)


def kernel(
    margin, chosen, cos_hbm, sin_hbm, q_hbm, k_hbm, da_hbm, x_hbm, wv_hbm,
    out_k, out_v,
    cosine, sine, q, k, da,
    xc, wc, probs, sc, qc, acc, vr, vals, dvb, dkb,
    pv, rz, va1, va2, va3, vb1, vb2, vb3,
    pa, ra1, ra2, qa, ra3,
    pb, rb1, rb2, qb, rb3,
    kz, rkz, send, recv, local, kz_send, kz_recv,
):
    rep, shard = lax.axis_index("rep"), lax.axis_index("shard")
    z, l, c = rep // 4, (rep // 2) % 2, rep % 2
    h, y = shard // 4, shard % 4
    x = 2 * h + l

    def dev(xx, yy, zz, cc):
        return (zz * 4 + (xx % 2) * 2 + cc, (xx // 2) * 4 + yy)

    def at_x(d):
        return dev((x + d) % 4, y, z, c)

    def at_y(d):
        return dev(x, (y + d) % 4, z, c)

    def at_z(d):
        return dev(x, y, (z + d) % 8, c)

    sib = dev(x, y, z, 1 - c)
    outer = dev(3 - x, y, z, c)
    inner = dev(2 * h + 1 - l, y, z, c)

    peers = [sib] + [at_x(d) for d in (1, 2, 3)] + [at_y(d) for d in (1, 2, 3)] + [at_z(d) for d in range(1, 8)]
    barrier = pltpu.get_barrier_semaphore()
    for peer in peers:
        pl.semaphore_signal(barrier, inc=1, device_id=peer, device_id_type=MESH)

    kept = []

    def keep(src, dst):
        copy = pltpu.make_async_copy(src, dst, local.at[len(kept)])
        copy.start()
        kept.append(copy)

    def rows_of(quarter):
        return pl.ds(pl.multiple_of(quarter * 512 + c * 256, 256), 256)

    def columns_of(xx, yy, core):
        return pl.ds(pl.multiple_of((xx // 2) * 4096 + yy * 1024 + (xx % 2) * 512 + core * 256, 256), 256)

    for src, dst in ((q_hbm, q), (k_hbm, k), (da_hbm, da), (cos_hbm, cosine), (sin_hbm, sine)):
        keep(src, dst)
    for xx in range(4):
        for yy in range(4):
            keep(x_hbm.at[:, columns_of(xx, yy, c)], xc.at[xx * 4 + yy, c])
    for quarter in range(2):
        keep(wv_hbm.at[rows_of(quarter)], wc.at[(2 * h + quarter) * 4 + y])

    pl.semaphore_wait(barrier, len(peers))

    links = Links(send, recv)
    first = 1 - l
    w_outer = {0: links.start(wv_hbm.at[rows_of(first)], wc.at[(2 * h + first) * 4 + y], outer)}
    w_y = {}
    for quarter in (first, l):
        for d in (1, 3, 2):
            w_y[d, quarter is first] = links.start(
                wv_hbm.at[rows_of(quarter)], wc.at[(2 * h + quarter) * 4 + y], at_y(d)
            )
    xs = []
    for xx in range(4):
        for yy in range(4):
            xs.append(links.start(x_hbm.at[:, columns_of(xx, yy, 1 - c)], xc.at[xx * 4 + yy, c], sib))

    strength = BETA_SPIN / (1.0 + jnp.exp(BETA_SPIN * margin[...]))
    weight = strength * (2 * chosen[...] - 1).astype(F32)
    s_pos = lax.broadcasted_iota(jnp.int32, (LEN, COLS), 0)
    t_pos = lax.broadcasted_iota(jnp.int32, (LEN, COLS), 1) % LEN
    allowed = s_pos <= t_pos
    for copy in kept[:5]:
        copy.wait()

    def forward(g):
        for seq in range(2):
            unit = 2 * g + seq
            rows = pl.ds(seq * LEN, LEN)
            w = weight if seq == 0 else -weight
            for head in range(GROUP):
                cols = pl.ds((g * GROUP + head) * HD, HD)
                span = pl.ds(head * LEN, LEN)
                qc[unit, span, :] = q[rows, cols]
                sc[unit, span, :] = (da[rows, cols].astype(F32) * w).astype(BF)
            kcols = pl.ds(g * HD, HD)
            scores = lax.dot_general(
                k[rows, kcols], qc[unit], (((1,), (1,)), ((), ())), preferred_element_type=F32
            ) * SCALE
            scores = jnp.where(allowed, scores, -jnp.inf)
            top = jnp.max(scores, axis=0, keepdims=True)
            expo = jnp.exp(scores - top)
            p = expo / jnp.sum(expo, axis=0, keepdims=True)
            probs[unit] = p
            dv = jnp.dot(p.astype(BF), sc[unit], preferred_element_type=F32)
            dvb[c, rows, kcols] = dv.astype(BF)

    for g in range(HEADS):
        forward(g)
    dv_copy = links.start(dvb.at[c], dvb.at[c], sib)
    for copy in kept[5:]:
        copy.wait()
    for copy in xs:
        copy.wait_recv()
    dv_copy.wait_recv()

    dt = jnp.transpose(dvb[...].reshape(2 * TOK, 512).astype(F32)).astype(BF)

    def grad_v(xx, carry):
        for yy in range(4):
            out = jnp.dot(dt, xc[xx * 4 + yy].reshape(2 * TOK, 256), preferred_element_type=F32).astype(BF)
            for zz in range(8):
                cb, rh = zz // 2, zz % 2
                pv[zz, xx, yy] = out[cb * 128 : (cb + 1) * 128, rh * 128 : (rh + 1) * 128]
        return carry

    lax.fori_loop(0, 4, grad_v, 0)

    half_a, half_b = pl.ds(0, 2), pl.ds(2, 2)

    def z_at(d):
        return pv.at[(z + d + 8) % 8]

    z_copies = {}

    def z_add(dst, src):
        for i in range(2):
            add_blocks(dst.at[i], src.at[i], 4)

    def z_step(step):
        for di, sign in ((0, 1), (1, -1)):
            lead, other = (half_a, half_b) if sign == 1 else (half_b, half_a)
            far = z_at(sign * (4 - step)).at[lead]
            near = z_at(sign * (3 - step)).at[other]
            if step > 0:
                z_copies[di, step - 1, 0].wait_recv()
                z_add(far, rz.at[di, step - 1, half_a])
            z_copies[di, step, 0] = links.start(far, rz.at[di, step, half_a], at_z(sign + 8))
            if step < 3:
                if step > 0:
                    z_copies[di, step - 1, 1].wait_recv()
                    z_add(near, rz.at[di, step - 1, half_b])
                z_copies[di, step, 1] = links.start(near, rz.at[di, step, half_b], at_z(sign + 8))

    z_step(0)

    def product(tokens, indices):
        total = None
        for j in indices:
            left = xc[j].reshape(2 * TOK, 256) if tokens is None else xc[j, tokens]
            part = jnp.dot(left, wc[j], preferred_element_type=F32)
            total = part if total is None else total + part
        return total

    def pass_outer(d):
        w_y[d, True].wait_recv()
        block = wc.at[(2 * h + first) * 4 + (y + 4 - d) % 4]
        w_outer[d] = []
        parts = 4 if d == 2 else 2
        for part in range(parts):
            piece = block.at[pl.ds(part * (256 // parts), 256 // parts)]
            w_outer[d].append(links.start(piece, piece, outer))

    w_inner = []

    def pass_inner(d):
        block = wc.at[(2 * (1 - h) + l) * 4 + (y + 4 - d) % 4]
        copies = w_outer[d] if d else [w_outer[0]]
        for part, copy in enumerate(copies):
            copy.wait_recv()
            size = 256 // len(copies)
            piece = block.at[pl.ds(part * size, size)]
            w_inner.append(links.start(piece, piece, inner))

    pass_outer(1)
    pass_outer(3)
    pass_inner(0)
    acc[...] = product(None, [(2 * h + i) * 4 + y for i in range(2)]).reshape(2, TOK, 512)
    pass_outer(2)
    pass_inner(1)
    z_step(1)
    pass_inner(3)
    for d in (1, 3, 2):
        w_y[d, False].wait_recv()
    acc[...] += product(
        None, [(2 * h + i % 2) * 4 + (y + 1 + i // 2) % 4 for i in range(6)]
    ).reshape(2, TOK, 512)
    pass_inner(2)
    acc[...] += product(None, [(2 * (1 - h) + l) * 4 + i for i in range(4)]).reshape(2, TOK, 512)
    for copy in w_inner:
        copy.wait_recv()
    last = [(2 * (1 - h) + 1 - l) * 4 + i for i in range(4)]
    acc[1 - c] += product(1 - c, last)
    value_copy = links.start(acc.at[1 - c], vr, sib)
    acc[c] += product(c, last)
    z_step(2)
    value_copy.wait_recv()
    vals[...] = (acc[c] + vr[...]).astype(BF)

    dk_copies = {}

    def backward(g):
        kcols = pl.ds(g * HD, HD)
        for seq in range(2):
            unit = 2 * g + seq
            rows = pl.ds(seq * LEN, LEN)
            dp = lax.dot_general(
                vals[rows, kcols], sc[unit], (((1,), (1,)), ((), ())), preferred_element_type=F32
            )
            p = probs[unit]
            mean = jnp.sum(p * dp, axis=0, keepdims=True)
            ds = (p * (dp - mean) * SCALE).astype(BF)
            rot = jnp.dot(ds, qc[unit], preferred_element_type=F32)
            swapped = jnp.concatenate([rot[:, HD // 2 :], rot[:, : HD // 2]], axis=1)
            dkb[g, c, rows, :] = (rot * cosine[...] + swapped * sine[...]).astype(BF)
        dk_copies[g] = links.start(dkb.at[g, c], dkb.at[g, c], sib)

    def grad_k(g):
        dk_copies[g].wait_recv()
        dt = jnp.transpose(dkb[g].reshape(2 * TOK, HD).astype(F32)).astype(BF)
        for i in range(16):
            out = jnp.dot(dt, xc[i].reshape(2 * TOK, 256), preferred_element_type=F32).astype(BF)
            for rh in range(2):
                pa[g, i // 4, i % 4, rh] = out[:64, rh * 128 : (rh + 1) * 128]
                pb[g, i % 4, i // 4, rh] = out[64:, rh * 128 : (rh + 1) * 128]

    stream_a = (at_x, x, pa, ra1, ra2, qa, at_y, y, ra3)
    stream_b = (at_y, y, pb, rb1, rb2, qb, at_x, x, rb3)
    lo, hi = pl.ds(0, 2), pl.ds(2, 2)
    ring = {}

    def ring_start(g):
        for name, (at, me, p, r1, r2, _, _, _, _) in (("a", stream_a), ("b", stream_b)):
            far = p.at[g, (me + 2) % 4]
            ring[g, name, "up1"] = links.start(far.at[lo], r1.at[g, 0], at(1))
            ring[g, name, "down1"] = links.start(far.at[hi], r1.at[g, 1], at(3))
        for name, (at, me, p, r1, r2, _, _, _, _) in (("a", stream_a), ("b", stream_b)):
            up, down = p.at[g, (me + 1) % 4], p.at[g, (me + 3) % 4]
            ring[g, name, "up2"] = links.start(up.at[hi], r2.at[g, 0, hi], at(1))
            ring[g, name, "down2"] = links.start(down.at[lo], r2.at[g, 1, lo], at(3))

    def ring_pass(g):
        for name, (at, me, p, r1, r2, _, _, _, _) in (("a", stream_a), ("b", stream_b)):
            up, down = p.at[g, (me + 1) % 4].at[lo], p.at[g, (me + 3) % 4].at[hi]
            ring[g, name, "up1"].wait_recv()
            for i in range(2):
                add_blocks(up.at[i], r1.at[g, 0, i], 2)
            ring[g, name, "up3"] = links.start(up, r2.at[g, 0, lo], at(1))
            ring[g, name, "down1"].wait_recv()
            for i in range(2):
                add_blocks(down.at[i], r1.at[g, 1, i], 2)
            ring[g, name, "down3"] = links.start(down, r2.at[g, 1, hi], at(3))

    def ring_end(g):
        for name, (_, me, p, _, r2, total, at, other, r3) in (("a", stream_a), ("b", stream_b)):
            for part in ("up2", "down2", "up3", "down3"):
                ring[g, name, part].wait_recv()
            for i in range(4):
                total[g, i] = (p[g, me, i].astype(F32) + r2[g, 0, i].astype(F32) + r2[g, 1, i].astype(F32)).astype(BF)
            for d in (2, 1, 3):
                ring[g, name, d] = links.start(total.at[g, (other + d) % 4], r3.at[g, d - 1], at(d))

    def plane_copy(zz):
        away = (zz - z + 8) % 8
        slot = (away + 7) % 8
        return pltpu.make_async_remote_copy(
            src_ref=kz.at[zz],
            dst_ref=rkz.at[slot],
            send_sem=kz_send.at[zz],
            recv_sem=kz_recv.at[slot],
            device_id=dev(x, y, zz, c),
            device_id_type=MESH,
        )

    def ring_last(g):
        for name, (_, _, _, _, _, total, _, other, r3) in (("a", stream_a), ("b", stream_b)):
            for d in (1, 2, 3):
                ring[g, name, d].wait_recv()
            mine = total[g, other].astype(F32)
            for d in range(3):
                mine += r3[g, d].astype(F32)
            rows = pl.ds(0, 64) if name == "a" else pl.ds(64, 64)
            kz[pl.ds(2 * g, 2), rows, :] = mine.astype(BF)
        for zz in (2 * g, 2 * g + 1):

            @pl.when(z != zz)
            def _():
                plane_copy(zz).start()

    def spot(ref, zz, ll, cc):
        row = ll * 512 + cc * 256 + (zz % 2) * 128
        return ref.at[
            pl.ds(pl.multiple_of(row, 128), 128), pl.ds(pl.multiple_of((zz // 2) * 128, 128), 128)
        ]

    def gather_start(ref, total):
        place = spot(ref, z, l, c)
        place[...] = jnp.transpose(total).astype(BF)
        state = {"z": {}, "in": {}, "sib": {}}
        for d in (4, 3, 5, 2, 6, 1, 7):
            state["z"][d] = links.start(place, place, at_z(d))
        state["in"][0] = links.start(place, place, inner)
        state["sib"][0, 0] = links.start(place, place, sib)
        return state

    def gather_mid(ref, state):
        for d in (1, 7, 2, 6, 3, 5, 4):
            state["z"][d].wait_recv()
            place = spot(ref, (z + 8 - d) % 8, l, c)
            state["in"][d] = links.start(place, place, inner)
            state["sib"][d, 0] = links.start(place, place, sib)

    def gather_end(ref, state):
        for d in (0, 1, 7, 2, 6, 3, 5, 4):
            state["in"][d].wait_recv()
            place = spot(ref, (z + 8 - d) % 8, 1 - l, c)
            state["sib"][d, 1] = links.start(place, place, sib)

    top, low = pl.ds(0, 64), pl.ds(64, 64)
    v_block = z_at(0)
    v_copies = {}

    def v_first():
        for di in (0, 1):
            z_copies[di, 2, 1].wait_recv()
            z_copies[di, 3, 0].wait_recv()
        for xx in range(4):
            up = rz.at[0, 3, xx] if xx < 2 else rz.at[0, 2, xx]
            down = rz.at[1, 2, xx + 2] if xx < 2 else rz.at[1, 3, xx - 2]
            for yy in range(4):
                v_block[xx, yy] = (v_block[xx, yy].astype(F32) + up[yy].astype(F32) + down[yy].astype(F32)).astype(BF)
        for d in (2, 1, 3):
            v_copies["a", d] = links.start(v_block.at[(x + d) % 4, :, top], va1.at[d - 1], at_x(d))
            v_copies["b", d] = links.start(v_block.at[:, (y + d) % 4, low], vb1.at[d - 1], at_y(d))

    def v_wait():
        for d in (1, 2, 3):
            v_copies["a", d].wait_recv()
            v_copies["b", d].wait_recv()

    def v_second():
        v_wait()
        for i in range(4):
            total_a = v_block[x, i, top].astype(F32)
            total_b = v_block[i, y, low].astype(F32)
            for d in range(3):
                total_a += va1[d, i].astype(F32)
                total_b += vb1[d, i].astype(F32)
            va2[i] = total_a.astype(BF)
            vb2[i] = total_b.astype(BF)
        for d in (2, 1, 3):
            v_copies["a", d] = links.start(va2.at[(y + d) % 4], va3.at[d - 1], at_y(d))
            v_copies["b", d] = links.start(vb2.at[(x + d) % 4], vb3.at[d - 1], at_x(d))

    def v_third():
        v_wait()
        total_a, total_b = va2[y].astype(F32), vb2[x].astype(F32)
        for d in range(3):
            total_a += va3[d].astype(F32)
            total_b += vb3[d].astype(F32)
        return gather_start(out_v, jnp.concatenate([total_a, total_b], axis=0))

    backward(0)
    backward(1)
    grad_k(0)
    ring_start(0)
    backward(2)
    grad_k(1)
    ring_start(1)
    ring_pass(0)
    backward(3)
    grad_k(2)
    ring_start(2)
    ring_pass(1)
    grad_k(3)
    ring_start(3)
    z_step(3)
    ring_pass(2)
    ring_pass(3)
    ring_end(0)
    ring_end(1)
    ring_last(0)
    v_first()
    ring_end(2)
    ring_last(1)
    ring_end(3)
    ring_last(2)
    v_second()
    ring_last(3)
    gv = v_third()
    total_k = kz[z].astype(F32)
    for slot in range(7):
        pltpu.make_async_remote_copy(
            src_ref=kz.at[0], dst_ref=rkz.at[slot], send_sem=kz_send.at[0], recv_sem=kz_recv.at[slot],
            device_id=sib, device_id_type=MESH,
        ).wait_recv()
        total_k += rkz[slot].astype(F32)
    gk = gather_start(out_k, total_k)
    gather_mid(out_v, gv)
    gather_mid(out_k, gk)
    gather_end(out_v, gv)
    gather_end(out_k, gk)
    for state in (gv, gk):
        for copy in state["sib"].values():
            copy.wait_recv()
    for copy in links.all:
        copy.wait_send()
    for zz in range(8):

        @pl.when(z != zz)
        def _():
            plane_copy(zz).wait_send()


def widen(k_ref, v_ref, k_out, v_out):
    k_out[...] = k_ref[...].astype(F32)
    v_out[...] = v_ref[...].astype(F32)


def rotary_tables():
    half = HD // 2
    freqs = np.float32(ROPE_BASE) ** (-2.0 * np.arange(half, dtype=np.float32) / HD)
    angles = np.arange(LEN, dtype=np.float32)[:, None] * freqs.astype(np.float32)[None, :]
    cosine, sine = np.cos(angles), np.sin(angles)
    return (
        np.concatenate([cosine, cosine], axis=1).astype(np.float32),
        np.concatenate([sine, -sine], axis=1).astype(np.float32),
    )


def shards(hidden_in, queries, keys, d_attn, value_weight, pair_margin, pair_chosen):
    cosine, sine = rotary_tables()
    vmem = pl.BlockSpec(memory_space=pltpu.VMEM)
    anywhere = pl.BlockSpec(memory_space=pl.ANY)
    block = (128, 128)
    key_grad, value_grad = pl.pallas_call(
        kernel,
        name="projection_grads",
        out_shape=[jax.ShapeDtypeStruct((1024, 512), BF)] * 2,
        in_specs=[vmem] * 2 + [anywhere] * 7,
        out_specs=[vmem] * 2,
        scratch_shapes=[
            pltpu.VMEM((LEN, HD), F32),
            pltpu.VMEM((LEN, HD), F32),
            pltpu.VMEM((TOK, 4096), BF),
            pltpu.VMEM((TOK, 512), BF),
            pltpu.VMEM((TOK, 4096), BF),
            pltpu.VMEM((16, 2, TOK, 256), BF),
            pltpu.VMEM((16, 256, 512), BF),
            pltpu.VMEM((8, LEN, COLS), F32),
            pltpu.VMEM((8, COLS, HD), BF),
            pltpu.VMEM((8, COLS, HD), BF),
            pltpu.VMEM((2, TOK, 512), F32),
            pltpu.VMEM((TOK, 512), F32),
            pltpu.VMEM((TOK, 512), BF),
            pltpu.VMEM((2, TOK, 512), BF),
            pltpu.VMEM((4, 2, TOK, HD), BF),
            pltpu.VMEM((8, 4, 4) + block, BF),
            pltpu.VMEM((2, 4, 4, 4) + block, BF),
        ]
        + [
            pltpu.VMEM((3, 4, 64, 128), BF),
            pltpu.VMEM((4, 64, 128), BF),
            pltpu.VMEM((3, 64, 128), BF),
        ]
        * 2
        + [
            pltpu.VMEM((4, 4, 4, 2, 64, 128), BF),
            pltpu.VMEM((4, 2, 2, 2, 64, 128), BF),
            pltpu.VMEM((4, 2, 4, 2, 64, 128), BF),
            pltpu.VMEM((4, 4, 2, 64, 128), BF),
            pltpu.VMEM((4, 3, 2, 64, 128), BF),
        ]
        * 2
        + [
            pltpu.VMEM((8,) + block, BF),
            pltpu.VMEM((7,) + block, BF),
            pltpu.SemaphoreType.DMA((260,)),
            pltpu.SemaphoreType.DMA((260,)),
            pltpu.SemaphoreType.DMA((23,)),
            pltpu.SemaphoreType.DMA((8,)),
            pltpu.SemaphoreType.DMA((7,)),
        ],
        compiler_params=pltpu.CompilerParams(
            collective_id=0, has_side_effects=True, vmem_limit_bytes=58 * 2**20
        ),
    )(
        pair_margin.reshape(1, 1),
        pair_chosen.reshape(1, 1),
        jnp.asarray(cosine),
        jnp.asarray(sine),
        queries,
        keys,
        d_attn,
        hidden_in,
        value_weight,
    )
    part = pl.BlockSpec((512, 512), lambda i: (i, 0))
    return pl.pallas_call(
        widen,
        name="widen",
        grid=(2,),
        out_shape=[jax.ShapeDtypeStruct((1024, 512), F32)] * 2,
        in_specs=[part] * 2,
        out_specs=[part] * 2,
    )(key_grad, value_grad)


def solution(mesh):
    placed = (
        P(("rep", "shard"), None),
        P(("rep", "shard"), None),
        P(("rep", "shard"), None),
        P(("rep", "shard"), None),
        P("shard", None),
        P(("rep", "shard")),
        P(("rep", "shard")),
    )
    return jax.shard_map(
        shards,
        mesh=mesh,
        in_specs=placed,
        out_specs=(P("shard", None), P("shard", None)),
        check_vma=False,
    )
```

time: 126 us -> 113 us (0.90)
  Pallas kernels: 120 us -> 111 us
  other arithmetic: 4.54 us -> 0 us
    pallas_call x1, Pallas kernels: 120 us -> 108 us  [shards(): pl.pallas_call(kernel, name='projection_grads', out_shape=[jax.ShapeDtype...]
    convert_element_type x2 -> x0, other arithmetic: 4.54 us -> none  [shards(): return (key_grad.astype(F32), value_grad.astype(F32))]
    pallas_call x0 -> x1, Pallas kernels: none -> 3.31 us  [shards(): pl.pallas_call(widen, name='widen', grid=(2,), out_shape=[jax.ShapeDtypeS...]
where the time goes in v2:
time: 113 us
  Pallas kernels  111 us (98%)
  between operations  1.93 us (2%)
    pallas_call x1, Pallas kernels, shards(): pl.pallas_call(kernel, name='projection_grads', out_shape=[jax.ShapeDtype...  108 us
    pallas_call x1, Pallas kernels, shards(): pl.pallas_call(widen, name='widen', grid=(2,), out_shape=[jax.ShapeDtypeS...  3.31 us

profile of v2, /device:TPU:1, one launch (start us, length us, event | category | flops | bytes accessed | tf_op | source)
XLA Modules:
  0.0 113.3 jit_solution(5288160253962638808)
XLA Ops:
  1.9 108.0 %projection_grads.1 = (bf16[1024,512]{1,0:T(8,128)(2,1)}, bf16[1024,512]{1,0:T(8,128)(2,1)}) custom-call(f32[1,1]{1,0:T(1,128)} %bitcast.2.margin, s32[1,1]{1,0:T(1,128)} %bitcast.3.chosen, f32[96,128]{1,0:T(8,128)} %constant.4.clone.cos_hbm, f32[96,128]{1,0:T(8,128)} %constant.5.clone.sin_hbm, bf16[192,4096]{1,0:T(8,128)(2,1)} %q_hbm.1, ...), custom_call_target="tpu_custom_call" | custom-call | tf_op jit(solution)/shard_map/projection_grads/pallas_call | solution.py:491
  110.0 3.3 %widen.1 = (f32[1024,512]{1,0:T(8,128)}, f32[1024,512]{1,0:T(8,128)}) custom-call(bf16[1024,512]{1,0:T(8,128)(2,1)} %get-tuple-element.4.k_ref, bf16[1024,512]{1,0:T(8,128)(2,1)} %get-tuple-element.5.v_ref), custom_call_target="tpu_custom_call" | custom-call | tf_op jit(solution)/shard_map/widen/pallas_call | solution.py:554

commit v3 on v2

--- a/solution.py
+++ b/solution.py
@@ -352,7 +352,7 @@
         place = spot(ref, z, l, c)
         place[...] = jnp.transpose(total).astype(BF)
         state = {"z": {}, "in": {}, "sib": {}}
-        for d in (4, 3, 5, 2, 6, 1, 7):
+        for d in (1, 7, 2, 6, 3, 5, 4):
             state["z"][d] = links.start(place, place, at_z(d))
         state["in"][0] = links.start(place, place, inner)
         state["sib"][0, 0] = links.start(place, place, sib)
@@ -429,19 +429,19 @@
     ring_pass(1)
     grad_k(3)
     ring_start(3)
+    ring_pass(2)
     z_step(3)
-    ring_pass(2)
     ring_pass(3)
     ring_end(0)
     ring_end(1)
     ring_last(0)
-    v_first()
     ring_end(2)
     ring_last(1)
     ring_end(3)
+    v_first()
     ring_last(2)
+    ring_last(3)
     v_second()
-    ring_last(3)
     gv = v_third()
     total_k = kz[z].astype(F32)
     for slot in range(7):
@@ -467,9 +467,17 @@
             plane_copy(zz).wait_send()
 
 
-def widen(k_ref, v_ref, k_out, v_out):
-    k_out[...] = k_ref[...].astype(F32)
-    v_out[...] = v_ref[...].astype(F32)
+def widen(k_ref, v_ref, k_out, v_out, k_wide, v_wide, sems):
+    copies = []
+    for part in range(2):
+        rows = pl.ds(part * 512, 512)
+        for i, (ref, wide, out) in enumerate(((k_ref, k_wide, k_out), (v_ref, v_wide, v_out))):
+            wide[rows, :] = ref[rows, :].astype(F32)
+            copy = pltpu.make_async_copy(wide.at[rows], out.at[rows], sems.at[part, i])
+            copy.start()
+            copies.append(copy)
+    for copy in copies:
+        copy.wait()
 
 
 def rotary_tables():
@@ -486,12 +494,12 @@
 def shards(hidden_in, queries, keys, d_attn, value_weight, pair_margin, pair_chosen):
     cosine, sine = rotary_tables()
     vmem = pl.BlockSpec(memory_space=pltpu.VMEM)
-    anywhere = pl.BlockSpec(memory_space=pl.ANY)
+    anywhere = pl.BlockSpec(memory_space=pltpu.HBM)
     block = (128, 128)
     key_grad, value_grad = pl.pallas_call(
         kernel,
         name="projection_grads",
-        out_shape=[jax.ShapeDtypeStruct((1024, 512), BF)] * 2,
+        out_shape=[pltpu.VMEM((1024, 512), BF)] * 2,
         in_specs=[vmem] * 2 + [anywhere] * 7,
         out_specs=[vmem] * 2,
         scratch_shapes=[
@@ -537,7 +545,7 @@
             pltpu.SemaphoreType.DMA((7,)),
         ],
         compiler_params=pltpu.CompilerParams(
-            collective_id=0, has_side_effects=True, vmem_limit_bytes=58 * 2**20
+            collective_id=0, has_side_effects=True, vmem_limit_bytes=56 * 2**20
         ),
     )(
         pair_margin.reshape(1, 1),
@@ -550,14 +558,16 @@
         hidden_in,
         value_weight,
     )
-    part = pl.BlockSpec((512, 512), lambda i: (i, 0))
+    key_grad = pltpu.with_memory_space_constraint(key_grad, pltpu.VMEM)
+    value_grad = pltpu.with_memory_space_constraint(value_grad, pltpu.VMEM)
     return pl.pallas_call(
         widen,
         name="widen",
-        grid=(2,),
         out_shape=[jax.ShapeDtypeStruct((1024, 512), F32)] * 2,
-        in_specs=[part] * 2,
-        out_specs=[part] * 2,
+        in_specs=[vmem] * 2,
+        out_specs=[anywhere] * 2,
+        scratch_shapes=[pltpu.VMEM((1024, 512), F32)] * 2 + [pltpu.SemaphoreType.DMA((2, 2))],
+        compiler_params=pltpu.CompilerParams(vmem_limit_bytes=40 * 2**20),
     )(key_grad, value_grad)
 
 

time: 113 us -> 109 us (0.965)
  Pallas kernels: 111 us -> 107 us
    pallas_call x2, Pallas kernels: 111 us -> 107 us  [the longest x1 105 us: shards(): pl.pallas_call(kernel, name='projection_grads', out_shape=[pltpu.VMEM((10...]
where the time goes in v3:
time: 109 us
  Pallas kernels  107 us (98%)
  between operations  2.09 us (2%)
    pallas_call x1, Pallas kernels, shards(): pl.pallas_call(kernel, name='projection_grads', out_shape=[pltpu.VMEM((10...  105 us

profile of v3, /device:TPU:1, one launch (start us, length us, event | category | flops | bytes accessed | tf_op | source)
XLA Modules:
  0.0 109.3 jit_solution(7651744199203239873)
XLA Ops:
  1.9 105.1 %projection_grads.1 = (bf16[1024,512]{1,0:T(8,128)(2,1)S(1)}, bf16[1024,512]{1,0:T(8,128)(2,1)S(1)}) custom-call(f32[1,1]{1,0:T(1,128)} %bitcast.2.margin, s32[1,1]{1,0:T(1,128)} %bitcast.3.chosen, f32[96,128]{1,0:T(8,128)} %constant.4.clone.cos_hbm, f32[96,128]{1,0:T(8,128)} %constant.5.clone.sin_hbm, bf16[192,4096]{1,0:T(8,128)(2,1)} %q_hbm.1, ...), custom_call_target="tpu_custom_call" | custom-call | tf_op jit(solution)/shard_map/projection_grads/pallas_call | solution.py:499
  107.0 2.1 %widen.1 = (f32[1024,512]{1,0:T(8,128)}, f32[1024,512]{1,0:T(8,128)}) custom-call(bf16[1024,512]{1,0:T(8,128)(2,1)S(1)} %get-tuple-element.4.k_ref, bf16[1024,512]{1,0:T(8,128)(2,1)S(1)} %get-tuple-element.5.v_ref), custom_call_target="tpu_custom_call" | custom-call | tf_op jit(solution)/shard_map/widen/pallas_call | solution.py:563

commit v4 on v3

--- a/solution.py
+++ b/solution.py
@@ -169,8 +169,6 @@
                 pv[zz, xx, yy] = out[cb * 128 : (cb + 1) * 128, rh * 128 : (rh + 1) * 128]
         return carry
 
-    lax.fori_loop(0, 4, grad_v, 0)
-
     half_a, half_b = pl.ds(0, 2), pl.ds(2, 2)
 
     def z_at(d):
@@ -197,7 +195,12 @@
                     z_add(near, rz.at[di, step - 1, half_b])
                 z_copies[di, step, 1] = links.start(near, rz.at[di, step, half_b], at_z(sign + 8))
 
-    z_step(0)
+    lax.fori_loop(0, 2, grad_v, 0)
+    z_copies[0, 0, 0] = links.start(z_at(4).at[half_a], rz.at[0, 0, half_a], at_z(9))
+    z_copies[1, 0, 1] = links.start(z_at(-3).at[half_a], rz.at[1, 0, half_b], at_z(7))
+    lax.fori_loop(2, 4, grad_v, 0)
+    z_copies[1, 0, 0] = links.start(z_at(-4).at[half_b], rz.at[1, 0, half_a], at_z(7))
+    z_copies[0, 0, 1] = links.start(z_at(3).at[half_b], rz.at[0, 0, half_b], at_z(9))
 
     def product(tokens, indices):
         total = None

time: 109 us -> 108 us (level)
  no operation moved by 1% of the time
where the time goes in v4:
time: 108 us
  Pallas kernels  106 us (98%)
  between operations  2.09 us (2%)
    pallas_call x1, Pallas kernels, shards(): pl.pallas_call(kernel, name='projection_grads', out_shape=[pltpu.VMEM((10...  104 us

profile of v4, /device:TPU:1, one launch (start us, length us, event | category | flops | bytes accessed | tf_op | source)
XLA Modules:
  0.0 108.3 jit_solution(17415929352957100560)
XLA Ops:
  1.9 104.1 %projection_grads.1 = (bf16[1024,512]{1,0:T(8,128)(2,1)S(1)}, bf16[1024,512]{1,0:T(8,128)(2,1)S(1)}) custom-call(f32[1,1]{1,0:T(1,128)} %bitcast.2.margin, s32[1,1]{1,0:T(1,128)} %bitcast.3.chosen, f32[96,128]{1,0:T(8,128)} %constant.4.clone.cos_hbm, f32[96,128]{1,0:T(8,128)} %constant.5.clone.sin_hbm, bf16[192,4096]{1,0:T(8,128)(2,1)} %q_hbm.1, ...), custom_call_target="tpu_custom_call" | custom-call | tf_op jit(solution)/shard_map/projection_grads/pallas_call | solution.py:502
  106.0 2.1 %widen.1 = (f32[1024,512]{1,0:T(8,128)}, f32[1024,512]{1,0:T(8,128)}) custom-call(bf16[1024,512]{1,0:T(8,128)(2,1)S(1)} %get-tuple-element.4.k_ref, bf16[1024,512]{1,0:T(8,128)(2,1)S(1)} %get-tuple-element.5.v_ref), custom_call_target="tpu_custom_call" | custom-call | tf_op jit(solution)/shard_map/widen/pallas_call | solution.py:566
